TPU v7x, 128 devices: a whole 4x4x4 slice. The times are simulated.
128 devices in a mesh: dp: 8 (over z_lo, x), tensor: 16 (over y, z_hi, core).
Axes of the slice: x: 4, y: 4, z: 4 (z_hi: 2, z_lo: 2; z = z_hi * 2 + z_lo), core: 2. Of those that a mesh axis runs over, the one named last changes fastest.
Arguments:
- activations: bfloat16 [8192, 4096], P('dp'), may hold values from -23 to 23
- out_grads: bfloat16 [8192, 16384], P('dp', 'tensor'), may hold values from -23 to 23
- input_basis: bfloat16 [4, 1024, 1024], P(None, 'tensor'), may hold values from -0.1875 to 0.1875
- output_basis: bfloat16 [16, 1024, 1024], P('tensor'), may hold values from -0.1875 to 0.1875
Outputs:
- scaling: float32 [4096, 16384], P('dp', 'tensor')
All inputs are finite; a program needn't handle non-finite values.
Results may differ from a plain program's by a relative error of at most 0.00031.
Values may be sent and summed in bfloat16 or wider, within the bound.
A program may use at most 128 MiB of HBM per device.

v0:
```python
import jax
import jax.numpy as jnp
from jax import lax
from jax.sharding import PartitionSpec as P


def per_device(activations, out_grads, input_basis, output_basis):
    tok_rows = activations.shape[0]
    num_blocks = input_basis.shape[0]
    block_width = input_basis.shape[2]
    act_blocks = activations.reshape(tok_rows, num_blocks, block_width)
    turned = jnp.einsum(
        "bji,tbi->bjt",
        lax.all_gather(input_basis, "tensor", axis=1, tiled=True),
        act_blocks,
        preferred_element_type=jnp.float32,
    )
    squares_in = (turned * turned).astype(jnp.bfloat16)
    squares_in = squares_in.reshape(num_blocks * block_width, tok_rows)
    out_blocks = output_basis.shape[0]
    grad_blocks = out_grads.reshape(tok_rows, out_blocks, block_width)
    turned_out = jnp.einsum(
        "tbi,bji->tbj", grad_blocks, output_basis, preferred_element_type=jnp.float32
    )
    squares_out = (
        (turned_out * turned_out).astype(jnp.bfloat16).reshape(tok_rows, out_blocks * block_width)
    )
    summed = lax.psum_scatter(
        jnp.dot(squares_in, squares_out, preferred_element_type=jnp.float32),
        "dp",
        scatter_dimension=0,
        tiled=True,
    )
    return summed / (tok_rows * lax.axis_size("dp"))


def solution(mesh):
    return jax.shard_map(
        per_device,
        mesh=mesh,
        in_specs=(
            P("dp", None),
            P("dp", "tensor"),
            P(None, "tensor", None),
            P("tensor", None, None),
        ),
        out_specs=P("dp", "tensor"),
        check_vma=False,
    )
```

profile of v0, /device:TPU:0, one launch (start us, length us, event | category | flops | bytes accessed | tf_op | source)
XLA Modules:
  0.0 298.4 jit_solution(4899576544919160454)
XLA Ops:
  6.5 0.0 copy-start
  6.5 0.0 all-gather.2.cloned.1.call-start
  6.5 0.7 all-gather.2.cloned.1.call-update
  7.3 0.0 reduce-scatter.2.cloned.1.call-start
  7.3 77.8 %all-gather.2.cloned.1.call-done = bf16[4,1024,1024]{2,1,0:T(8,128)(2,1)} async-done(((bf16[4,64,1024]{2,1,0:T(8,128)(2,1)}), bf16[4,1024,1024]{2,1,0:T(8,128)(2,1)}) %all-gather.2.cloned.1.call-update) | async-done | bytes 8388624 | tf_op jit(solution)/shard_map/all_gather | solution.py:14
  85.1 15.7 %multiply_convert_fusion = bf16[4,1024,1024]{2,1,0:T(8,128)(2,1)} fusion(bf16[4,1024,1024]{2,1,0:T(8,128)(2,1)} %all-gather.2.cloned.1.call-done, bf16[128,4,8,1024]{3,2,1,0:T(8,128)(2,1)} %bitcast.19), kind=kOutput, calls=%fused_computation | convolution fusion | flops 8598323200 | bytes 25165824 | tf_op jit(solution)/shard_map/bji,tbi->bjt/dot_general | solution.py:12
  100.9 0.0 copy-done
  100.9 18.3 %fusion.2 = f32[4096,1024]{1,0:T(8,128)} fusion(bf16[4096,1024]{1,0:T(8,128)(2,1)} %bitcast.20, bf16[1024,1024]{1,0:T(8,128)(2,1)S(1)} %copy-done, bf16[1,1024,1024]{2,1,0:T(8,128)(2,1)} %param.7), kind=kOutput, calls=%fused_computation.4 | convolution fusion | flops 10739515392 | bytes 29360128 | tf_op jit(solution)/shard_map/dot_general | solution.py:29
  119.2 0.0 reduce-scatter.2.cloned.1.call-update
  119.2 169.1 %reduce-scatter.2.cloned.1.call-done = f32[512,1024]{1,0:T(8,128)} async-done(((f32[4096,1024]{1,0:T(8,128)}), f32[512,1024]{1,0:T(8,128)}) %reduce-scatter.2.cloned.1.call-update) | async-done | bytes 2097168 | tf_op jit(solution)/shard_map/reduce_scatter | solution.py:28
  288.3 3.2 %broadcast_multiply_fusion = f32[512,1024]{1,0:T(8,128)} fusion(f32[512,1024]{1,0:T(8,128)} %reduce-scatter.2.cloned.1.call-done), kind=kLoop, calls=%fused_computation.7 | loop fusion | flops 524288 | bytes 4194304 | tf_op jit(solution)/shard_map/div | solution.py:34
Async XLA Ops:
  6.5 94.3 %copy-start = (bf16[1024,1024]{1,0:T(8,128)(2,1)S(1)}, bf16[1024,1024]{1,0:T(8,128)(2,1)}, u32[]{:S(2)}) copy-start(bf16[1024,1024]{1,0:T(8,128)(2,1)} %param.5) | copy-start | bytes 6291460
  6.5 78.6 %all-gather.2.cloned.1.call-start = ((), (), s32[]{:S(2)}) async-start(), calls=%async_computation.1 | async-start | bytes 8912896 | tf_op jit(solution)/shard_map/all_gather | solution.py:14
  7.3 281.1 %reduce-scatter.2.cloned.1.call-start = ((), (), s32[]{:S(2)}) async-start(), calls=%async_computation.2 | async-start | bytes 18874368 | tf_op jit(solution)/shard_map/reduce_scatter | solution.py:28
Sparse Core Ops, SparseCore 0:
  9.8 75.2 all-gather.1
  119.3 168.9 reduce-scatter.1
where the time goes:
time: 299 us; the launch traced here: 298 us
  waiting for transfers between devices  248 us (83%)
  matrix products  34.1 us (11%)
  between operations  13.4 us (4%)
  other arithmetic  3.22 us (1%)
    reduce_scatter x1, waiting for transfers between devices, per_device(): lax.psum_scatter(jnp.dot(squares_in, squares_out, preferred_element_type=...  169 us
    all_gather x1, waiting for transfers between devices, per_device(): lax.all_gather(input_basis, 'tensor', axis=1, tiled=True)  77.8 us
    dot_general x1, matrix products, per_device(): jnp.dot(squares_in, squares_out, preferred_element_type=jnp.float32)  18.3 us
    dot_general x1, matrix products, per_device(): jnp.einsum('bji,tbi->bjt', lax.all_gather(input_basis, 'tensor', axis=1,...  15.7 us
  transfers between devices with their start and end apart: 2, of which 2 were waited for; matrix products, arithmetic and copies ran while one was open for 0% of the time, Pallas kernels for 0%

commit v1 on v0

v1 whole, which is shorter than its diff:
```python
import functools

import jax
import jax.numpy as jnp
from jax import lax
from jax.experimental import pallas as pl
from jax.experimental.pallas import tpu as pltpu
from jax.sharding import PartitionSpec as P

MESH = pl.DeviceIdType.MESH
F32, BF16 = jnp.float32, jnp.bfloat16
LANES = 128
ROWS = 64
NBLK = 4
WIDTH = 1024
TILES = WIDTH // LANES
UNIT = TILES * ROWS + 16
SLICES = 16
FSLOTS = 8
LAST = SLICES + 6
TINY = float(2.0**-100)
UP = float(2.0**14)
FLOOR = float(2.0**-126)


def pick(index, values):
    out = values[-1]
    for at in range(len(values) - 2, -1, -1):
        out = jnp.where(index == at, values[at], out)
    return out


def flip(y, e):
    return lax.rem(y + e, 2) + 2 * lax.rem(y // 2 + e // 2, 2)


def encode(read, unit):
    top = read(0).reshape(ROWS // 8, 8, LANES).max(axis=0)
    for col in range(1, TILES):
        top = jnp.maximum(top, read(col).reshape(ROWS // 8, 8, LANES).max(axis=0))
    scale = jnp.maximum(top, TINY).astype(BF16).astype(F32)
    inv = UP / scale
    unit[pl.ds(TILES * ROWS, 16), :] = jnp.concatenate([scale, scale], axis=0).astype(BF16)
    for col in range(TILES):
        v = (read(col).reshape(ROWS // 8, 8, LANES) * inv).reshape(ROWS, LANES)
        v = v * v
        v = v * v
        v = v * v
        unit[pl.ds(col * ROWS, ROWS), :] = v.astype(BF16)


def decoder(unit):
    scale = unit[pl.ds(TILES * ROWS, 16), :].astype(F32)[0:8] * (1.0 / UP)

    def tile(col):
        v = jnp.maximum(unit[pl.ds(col * ROWS, ROWS), :].astype(F32), FLOOR)
        w = lax.rsqrt(lax.rsqrt(v))
        v = w * lax.rsqrt(w)
        return (v.reshape(ROWS // 8, 8, LANES) * scale).reshape(ROWS, LANES)

    return tile


def cols(col):
    return pl.ds(col * LANES, LANES)


def block_rows(b):
    return pl.ds(pl.multiple_of(b * ROWS, ROWS), ROWS)


def kernel(
    act_h, grad_h, ib_h, ob_h, out_h,
    act, grad, ib, ob, s_in, s_out, acc, xs, xr, zs, zr, out,
    ld_sem, a_ss, a_rs, x_ss, x_rs, z_ss, z_rs, o_sem,
):
    dp, t = lax.axis_index("dp"), lax.axis_index("tensor")
    x, zl = lax.rem(dp, 4), dp // 4
    y, zh, core = t // 4, lax.rem(t // 2, 2), lax.rem(t, 2)
    q, xh = lax.rem(x, 2), x // 2

    def dev(x=x, y=y, zl=zl, zh=zh, core=core):
        return (zl * 4 + x, y * 4 + zh * 2 + core)

    sibling = dev(core=1 - core)
    y1, y3 = dev(y=flip(y, 1)), dev(y=flip(y, 3))
    zfar = dev(zh=1 - zh)
    znear = dev(zl=1 - zl)
    side = [dev(x=2 * h + 1 - q) for h in range(2)]

    loads = [
        pltpu.make_async_copy(ib_h, ib, ld_sem.at[0]),
        pltpu.make_async_copy(act_h.at[:, pl.ds(0, WIDTH)], act.at[0], ld_sem.at[1]),
        pltpu.make_async_copy(act_h.at[:, pl.ds(WIDTH, WIDTH)], act.at[1], ld_sem.at[2]),
        pltpu.make_async_copy(act_h.at[:, pl.ds(2 * WIDTH, WIDTH)], act.at[2], ld_sem.at[3]),
        pltpu.make_async_copy(act_h.at[:, pl.ds(3 * WIDTH, WIDTH)], act.at[3], ld_sem.at[4]),
        pltpu.make_async_copy(ob_h.at[0], ob, ld_sem.at[5]),
        pltpu.make_async_copy(grad_h, grad, ld_sem.at[6]),
    ]
    for load in loads:
        load.start()
    barrier = pltpu.get_barrier_semaphore()
    partners = [sibling, y1, y3, zfar, znear] + side
    for partner in partners:
        pl.semaphore_signal(barrier, inc=1, device_id=partner, device_id_type=MESH)

    def half_of(tt, half):
        return s_in.at[tt, pl.ds(half * 2 * ROWS, 2 * ROWS)]

    def a_copy(tt, half, target, slot):
        return pltpu.make_async_remote_copy(
            src_ref=half_of(tt, half),
            dst_ref=half_of(tt, half),
            send_sem=a_ss.at[slot],
            recv_sem=a_rs.at[tt, half],
            device_id=target,
            device_id_type=MESH,
        )

    def a_wait(tt, half):
        pltpu.make_async_copy(half_of(tt, half), half_of(tt, half), a_rs.at[tt, half]).wait()

    loads[0].wait()
    for b in range(NBLK):
        loads[1 + b].wait()

        @pl.loop(0, 2)
        def _(j):
            part = pl.ds(pl.multiple_of(j * 512, 512), 512)
            turned = lax.dot_general(
                ib[b], act[b, part, :], (((1,), (1,)), ((), ())), preferred_element_type=F32
            )
            s_in[t, pl.ds(b * ROWS, ROWS), part] = (turned * turned).astype(BF16)

        if b == 1:
            pl.semaphore_wait(barrier, len(partners))
        if b % 2 == 1:
            half = b // 2
            for at, target in enumerate((y3, y1, zfar, sibling)):
                a_copy(t, half, target, half * 4 + at).start()
    loads[5].wait()
    loads[6].wait()

    @pl.loop(0, 4)
    def _(j):
        part = pl.ds(pl.multiple_of(j * 256, 256), 256)
        turned = lax.dot_general(
            grad[...], ob[part, :], (((1,), (1,)), ((), ())), preferred_element_type=F32
        )
        s_out[:, part] = (turned * turned).astype(BF16)

    def slice_at(s):
        group = s // 2
        e = pick(group, [0, 3, 0, 1, 3, 2, 1, 2])
        far = pick(group, [0, 0, 1, 0, 1, 0, 1, 1])
        yy = flip(y, e)
        tt = yy * 4 + lax.rem(zh + far, 2) * 2 + lax.rem(core + s, 2)
        return tt, (yy // 2) == q

    def slice_of(e, far):
        return flip(y, e) * 4 + lax.rem(zh + far, 2) * 2 + core

    def forward(e, far, targets, slot):
        tt = slice_of(e, far)
        for half in range(2):
            a_wait(tt, half)
            for target in targets[half]:
                a_copy(tt, half, target, slot).start()
                slot += 1
        return slot

    def forwards(event, slot):
        if event == 0:
            slot = forward(3, 0, [[sibling], [sibling, y1]], slot)
            slot = forward(1, 0, [[sibling, y3], [sibling]], slot)
            slot = forward(0, 1, [[y3, y1, sibling], [y3, y1, sibling]], slot)
        elif event == 1:
            slot = forward(3, 1, [[sibling], [sibling, y1]], slot)
            slot = forward(1, 1, [[sibling, y3], [sibling]], slot)
            slot = forward(2, 0, [[sibling], [sibling]], slot)
        else:
            slot = forward(2, 1, [[sibling], [sibling]], slot)
        return slot

    def x_copy(s, first, count, h):
        return pltpu.make_async_remote_copy(
            src_ref=xs.at[s, pl.ds(first, count)],
            dst_ref=xr.at[s, pl.ds(2 * xh, count)],
            send_sem=x_ss.at[s, h],
            recv_sem=x_rs.at[s, xh],
            device_id=side[h],
            device_id_type=MESH,
        )

    def x_wait(s, h, count):
        ref = xr.at[s, pl.ds(2 * h, count)]
        pltpu.make_async_copy(ref, ref, x_rs.at[s, h]).wait()

    def z_copy(s):
        return pltpu.make_async_remote_copy(
            src_ref=zs.at[s],
            dst_ref=zr.at[s],
            send_sem=z_ss.at[s],
            recv_sem=z_rs.at[s],
            device_id=znear,
            device_id_type=MESH,
        )

    def out_copy(s):
        tt, _ = slice_at(s)
        rows = pl.ds(pl.multiple_of(lax.rem(tt, 8) * ROWS, ROWS), ROWS)
        return pltpu.make_async_copy(out.at[rows], out_h.at[rows], o_sem.at[s])

    def reader(slot, b):
        return lambda col: acc[slot, block_rows(b), cols(col)]

    @pl.loop(0, LAST)
    def _(step):
        s2 = jnp.clip(step - 2, 0, SLICES - 1)
        _, own2 = slice_at(s2)

        @pl.when((step >= 2) & (step - 2 < SLICES) & jnp.logical_not(own2))
        def _():
            slot = lax.rem(s2, FSLOTS)
            for h in range(2):
                x_wait(s2, h, 1)
                tile = decoder(xr.at[s2, 2 * h])
                rows = block_rows(2 * xh + 1 - h)
                for col in range(TILES):
                    acc[slot, rows, cols(col)] += tile(col)
            for h in range(2):

                @pl.loop(0, 2)
                def _(zb):
                    encode(reader(slot, 2 * zb + h), xs.at[s2, 2 * h + zb])

                x_copy(s2, 2 * h, 2, h).start()

        s3 = jnp.clip(step - 4, 0, SLICES - 1)
        _, own3 = slice_at(s3)

        @pl.when((step >= 4) & (step - 4 < SLICES) & own3)
        def _():
            slot = lax.rem(s3, FSLOTS)
            for h in range(2):
                x_wait(s3, h, 2)

            @pl.loop(0, 2)
            def _(i):
                zb = lax.rem(1 - zl + i, 2)
                rows = block_rows(2 * zb + xh)
                tile0, tile1 = decoder(xr.at[s3, zb]), decoder(xr.at[s3, 2 + zb])
                for col in range(TILES):
                    acc[slot, rows, cols(col)] += tile0(col) + tile1(col)

                @pl.when(i == 0)
                def _():
                    encode(reader(slot, 2 * zb + xh), zs.at[s3])
                    z_copy(s3).start()

        s4 = jnp.clip(step - 6, 0, SLICES - 1)
        tt4, own4 = slice_at(s4)

        @pl.when((step >= 6) & own4)
        def _():
            slot = lax.rem(s4, FSLOTS)
            pltpu.make_async_copy(zr.at[s4], zr.at[s4], z_rs.at[s4]).wait()
            tile = decoder(zr.at[s4])
            rows = pl.ds(pl.multiple_of(lax.rem(tt4, 8) * ROWS, ROWS), ROWS)
            for col in range(TILES):
                both = acc[slot, block_rows(2 * zl + xh), cols(col)] + tile(col)
                out[rows, cols(col)] = both * (1.0 / 8192)
            out_copy(s4).start()

        for event, when in enumerate((2, 6, 11)):

            @pl.when(step == when)
            def _():
                forwards(event, (8, 20, 28)[event])

        s1 = jnp.clip(step, 0, SLICES - 1)
        tt1, own1 = slice_at(s1)

        @pl.when((step < SLICES) & (lax.rem(step, 2) == 1))
        def _():
            a_wait(tt1, 0)
            a_wait(tt1, 1)

        @pl.when(step < SLICES)
        def _():
            acc[lax.rem(s1, FSLOTS)] = jnp.dot(s_in[tt1], s_out[...], preferred_element_type=F32)

        @pl.when((step < SLICES) & own1)
        def _():
            slot = lax.rem(s1, FSLOTS)
            for zb in range(2):
                encode(reader(slot, 2 * zb + 1 - xh), xs.at[s1, zb])
                x_copy(s1, zb, 1, zb).start()

    @pl.loop(0, 32)
    def _(at):
        ref = half_of(t, 0)

        @pl.when(at < 30)
        def _():
            pltpu.make_async_copy(ref, ref, a_ss.at[at]).wait()

    @pl.loop(0, SLICES)
    def _(s):
        _, own = slice_at(s)

        @pl.when(own)
        def _():
            for h in range(2):
                ref = xs.at[s, pl.ds(0, 1)]
                pltpu.make_async_copy(ref, ref, x_ss.at[s, h]).wait()
            pltpu.make_async_copy(zs.at[s], zs.at[s], z_ss.at[s]).wait()
            out_copy(s).wait()

        @pl.when(jnp.logical_not(own))
        def _():
            for h in range(2):
                ref = xs.at[s, pl.ds(0, 2)]
                pltpu.make_async_copy(ref, ref, x_ss.at[s, h]).wait()


def per_device(activations, out_grads, input_basis, output_basis):
    any_spec = pl.BlockSpec(memory_space=pl.ANY)
    dma = pltpu.SemaphoreType.DMA
    return pl.pallas_call(
        kernel,
        out_shape=jax.ShapeDtypeStruct((8 * ROWS, WIDTH), F32),
        in_specs=[any_spec] * 4,
        out_specs=any_spec,
        scratch_shapes=[
            pltpu.VMEM((NBLK, 1024, WIDTH), BF16),
            pltpu.VMEM((1024, WIDTH), BF16),
            pltpu.VMEM((NBLK, ROWS, WIDTH), BF16),
            pltpu.VMEM((1024, WIDTH), BF16),
            pltpu.VMEM((SLICES, NBLK * ROWS, 1024), BF16),
            pltpu.VMEM((1024, WIDTH), BF16),
            pltpu.VMEM((FSLOTS, NBLK * ROWS, WIDTH), F32),
            pltpu.VMEM((SLICES, 4, UNIT, LANES), BF16),
            pltpu.VMEM((SLICES, 4, UNIT, LANES), BF16),
            pltpu.VMEM((SLICES, UNIT, LANES), BF16),
            pltpu.VMEM((SLICES, UNIT, LANES), BF16),
            pltpu.VMEM((8 * ROWS, WIDTH), F32),
            dma((7,)),
            dma((30,)),
            dma((SLICES, 2)),
            dma((SLICES, 2)),
            dma((SLICES, 2)),
            dma((SLICES,)),
            dma((SLICES,)),
            dma((SLICES,)),
        ],
        compiler_params=pltpu.CompilerParams(
            collective_id=0, has_side_effects=True, vmem_limit_bytes=60 * 2**20
        ),
        cost_estimate=pl.CostEstimate(
            flops=12 * 10**9, bytes_accessed=16 * 2**20, transcendentals=10**7
        ),
        name="scaling",
    )(activations, out_grads, input_basis, output_basis)


def solution(mesh):
    return jax.shard_map(
        per_device,
        mesh=mesh,
        in_specs=(
            P("dp", None),
            P("dp", "tensor"),
            P(None, "tensor", None),
            P("tensor", None, None),
        ),
        out_specs=P("dp", "tensor"),
        check_vma=False,
    )
```

time: 299 us -> 122 us (0.41)
  the two profiles are of different devices: /device:TPU:0 before, /device:TPU:6 now
where the time goes in v1:
time: 122 us
  Pallas kernels  118 us (97%)
  local copies, waits for them, and re-layouts  3.16 us (3%)
    pallas_call x1, Pallas kernels, per_device(): pl.pallas_call(kernel, out_shape=jax.ShapeDtypeStruct((8 * ROWS, WIDTH),...  118 us
    unnamed x1, local copies, waits for them, and re-layouts  3.16 us

profile of v1, /device:TPU:6, one launch (start us, length us, event | category | flops | bytes accessed | tf_op | source)
XLA Modules:
  0.0 121.5 jit_solution(12130987203426439104)
XLA Ops:
  0.0 118.4 %scaling.1 = f32[512,1024]{1,0:T(8,128)} custom-call(bf16[1024,4096]{1,0:T(8,128)(2,1)} %act_h.1, bf16[1024,1024]{1,0:T(8,128)(2,1)} %grad_h.1, bf16[4,64,1024]{2,1,0:T(8,128)(2,1)} %ib_h.1, bf16[1,1024,1024]{2,1,0:T(8,128)(2,1)} %ob_h.1), custom_call_target="tpu_custom_call" | custom-call | flops 12000000000 | bytes 16777216 | tf_op jit(solution)/shard_map/scaling/pallas_call | solution.py:330
  118.4 3.2 %copy.6 = f32[512,1024]{1,0:T(8,128)} copy(f32[512,1024]{1,0:T(8,128)} %scaling.1) | data formatting | bytes 4194304

commit v2 on v1

v2 whole, which is shorter than its diff:
```python
import functools

import jax
import jax.numpy as jnp
from jax import lax
from jax.experimental import pallas as pl
from jax.experimental.pallas import tpu as pltpu
from jax.sharding import PartitionSpec as P

MESH = pl.DeviceIdType.MESH
F32, BF16 = jnp.float32, jnp.bfloat16
LANES = 128
ROWS = 64
NBLK = 4
WIDTH = 1024
TILES = WIDTH // LANES
UNIT = TILES * ROWS + 16
HALF_UNIT = TILES // 2 * ROWS + 16
SLICES = 16
FSLOTS = 9
ORDER = [
    (0, 0, 1, 1),
    (0, 0, 0, 0),
    (3, 0, 0, 0),
    (1, 0, 0, 1),
    (1, 0, 1, 1),
    (3, 0, 1, 0),
    (0, 1, 0, 0),
    (2, 0, 0, 0),
    (2, 0, 1, 1),
    (0, 1, 1, 0),
    (3, 1, 1, 1),
    (3, 1, 0, 0),
    (1, 1, 1, 0),
    (2, 1, 1, 1),
    (2, 1, 0, 0),
    (1, 1, 0, 1),
]
LAGS = {
    ("X", 1): 2,
    ("X", 2): 7,
    ("X", 3): 8,
    ("Z", 1): 3,
    ("Z", 2): 6,
    ("Z", 3): 8,
}
EVENTS = [("a0", 2), ("a1", 2), ("z0", 1), ("z1", 6), ("b0", 8), ("b1", 8), ("c", 7), ("d", 12)]
SEQUENCE = (2, "ev", 0, 1, 3)
SLOTS = {"z0": 6, "z1": 9, "a0": 12, "a1": 15, "b0": 18, "b1": 21, "c": 24, "d": 26}
LAST = SLICES + max(LAGS.values())
TINY = float(2.0**-100)
UP = float(2.0**14)
FLOOR = float(2.0**-126)


def pick(index, values):
    out = values[-1]
    for at in range(len(values) - 2, -1, -1):
        out = jnp.where(index == at, values[at], out)
    return out


def flip(y, e):
    return lax.rem(y + e, 2) + 2 * lax.rem(y // 2 + e // 2, 2)


def encode(read, unit, tiles=tuple(range(TILES))):
    top = read(tiles[0]).reshape(ROWS // 8, 8, LANES).max(axis=0)
    for col in tiles[1:]:
        top = jnp.maximum(top, read(col).reshape(ROWS // 8, 8, LANES).max(axis=0))
    scale = jnp.maximum(top, TINY).astype(BF16).astype(F32)
    inv = UP / scale
    unit[pl.ds(len(tiles) * ROWS, 16), :] = jnp.concatenate([scale, scale], axis=0).astype(BF16)
    for at, col in enumerate(tiles):
        v = (read(col).reshape(ROWS // 8, 8, LANES) * inv).reshape(ROWS, LANES)
        v = v * v
        v = v * v
        v = v * v
        unit[pl.ds(at * ROWS, ROWS), :] = v.astype(BF16)


def decoder(unit, tiles=TILES):
    scale = unit[pl.ds(tiles * ROWS, 16), :].astype(F32)[0:8] * (1.0 / UP)

    def tile(col):
        v = jnp.maximum(unit[pl.ds(col * ROWS, ROWS), :].astype(F32), FLOOR)
        w = lax.rsqrt(lax.rsqrt(v))
        v = w * lax.rsqrt(w)
        return (v.reshape(ROWS // 8, 8, LANES) * scale).reshape(ROWS, LANES)

    return tile


def cols(col):
    return pl.ds(col * LANES, LANES)


def block_rows(b):
    return pl.ds(pl.multiple_of(b * ROWS, ROWS), ROWS)


def kernel(
    act_h, grad_h, ib_h, ob_h, out_h,
    act, grad, ib, ib_far, ob, s_in, s_out, acc, xs, xr, out,
    ld_sem, b_ss, b_rs, a_ss, a_rs, x_ss, x_rs, z_ss, z_rs, o_sem,
):
    dp, t = lax.axis_index("dp"), lax.axis_index("tensor")
    x, zl = lax.rem(dp, 4), dp // 4
    y, zh, core = t // 4, lax.rem(t // 2, 2), lax.rem(t, 2)
    q, xh = lax.rem(x, 2), x // 2

    def dev(x=x, y=y, zl=zl, zh=zh, core=core):
        return (zl * 4 + x, y * 4 + zh * 2 + core)

    sibling = dev(core=1 - core)
    y1, y3 = dev(y=flip(y, 1)), dev(y=flip(y, 3))
    zback = dev(zl=1 - zl, zh=1 - zh)
    znear = dev(zl=1 - zl)
    side = [dev(x=2 * h + 1 - q) for h in range(2)]

    loads = [
        pltpu.make_async_copy(ib_h, ib, ld_sem.at[0]),
        pltpu.make_async_copy(act_h.at[:, pl.ds(0, WIDTH)], act.at[0], ld_sem.at[1]),
        pltpu.make_async_copy(act_h.at[:, pl.ds(WIDTH, WIDTH)], act.at[1], ld_sem.at[2]),
        pltpu.make_async_copy(act_h.at[:, pl.ds(2 * WIDTH, WIDTH)], act.at[2], ld_sem.at[3]),
        pltpu.make_async_copy(act_h.at[:, pl.ds(3 * WIDTH, WIDTH)], act.at[3], ld_sem.at[4]),
        pltpu.make_async_copy(ob_h.at[0], ob, ld_sem.at[5]),
        pltpu.make_async_copy(grad_h, grad, ld_sem.at[6]),
    ]
    for load in loads:
        load.start()
    barrier = pltpu.get_barrier_semaphore()
    partners = [sibling, y1, y3, zback, znear] + side
    for partner in partners:
        pl.semaphore_signal(barrier, inc=1, device_id=partner, device_id_type=MESH)

    def half_of(tt, half):
        return s_in.at[tt, pl.ds(half * 2 * ROWS, 2 * ROWS)]

    def a_copy(tt, half, target, slot):
        return pltpu.make_async_remote_copy(
            src_ref=half_of(tt, half),
            dst_ref=half_of(tt, half),
            send_sem=a_ss.at[slot],
            recv_sem=a_rs.at[tt, half],
            device_id=target,
            device_id_type=MESH,
        )

    def a_wait(tt, half):
        pltpu.make_async_copy(half_of(tt, half), half_of(tt, half), a_rs.at[tt, half]).wait()

    def b_copy(half):
        return pltpu.make_async_remote_copy(
            src_ref=ib.at[pl.ds(2 * half, 2)],
            dst_ref=ib_far.at[pl.ds(2 * half, 2)],
            send_sem=b_ss.at[half],
            recv_sem=b_rs.at[half],
            device_id=zback,
            device_id_type=MESH,
        )

    def rotate(basis, b, tt):
        @pl.loop(0, 2)
        def _(j):
            part = pl.ds(pl.multiple_of(j * 512, 512), 512)
            turned = lax.dot_general(
                basis[b], act[b, part, :], (((1,), (1,)), ((), ())), preferred_element_type=F32
            )
            s_in[tt, block_rows(b), part] = (turned * turned).astype(BF16)

    loads[0].wait()
    for b in range(NBLK):
        loads[1 + b].wait()
        rotate(ib, b, t)
        if b == 0:
            pl.semaphore_wait(barrier, len(partners))
        if b % 2 == 1:
            half = b // 2
            for at, target in enumerate((y3, y1, sibling)):
                a_copy(t, half, target, half * 3 + at).start()
            b_copy(half).start()
    loads[5].wait()
    loads[6].wait()

    @pl.loop(0, 4)
    def _(j):
        part = pl.ds(pl.multiple_of(j * 256, 256), 256)
        turned = lax.dot_general(
            grad[...], ob[part, :], (((1,), (1,)), ((), ())), preferred_element_type=F32
        )
        s_out[:, part] = (turned * turned).astype(BF16)

    codes = [e + 4 * far + 8 * other + 16 * zfirst for e, far, other, zfirst in ORDER]

    def slice_at(s):
        code = pick(s, codes)
        yy = flip(y, lax.rem(code, 4))
        zz = lax.rem(zh + lax.rem(code // 4, 2), 2)
        tt = yy * 4 + zz * 2 + lax.rem(core + code // 8, 2)
        return tt, (yy // 2) == q, code // 16

    def slice_of(e, far):
        return flip(y, e) * 4 + lax.rem(zh + far, 2) * 2 + core

    def forward(e, far, half, targets, slot):
        tt = slice_of(e, far)
        a_wait(tt, half)
        for at, target in enumerate(targets):
            a_copy(tt, half, target, slot + at).start()

    def gather(event):
        slot = SLOTS[event]
        if event in ("z0", "z1"):
            half = int(event[1])
            ref = ib_far.at[pl.ds(2 * half, 2)]
            pltpu.make_async_copy(ref, ref, b_rs.at[half]).wait()
            tt = slice_of(0, 1)

            @pl.loop(0, 2)
            def _(i):
                rotate(ib_far, 2 * half + i, tt)

            for at, target in enumerate((y3, y1, sibling)):
                a_copy(tt, half, target, slot + at).start()
        elif event in ("a0", "b0"):
            far = int(event == "b0")
            forward(3, far, 0, [sibling], slot)
            forward(1, far, 0, [y3, sibling], slot + 1)
        elif event in ("a1", "b1"):
            far = int(event == "b1")
            forward(3, far, 1, [y1, sibling], slot)
            forward(1, far, 1, [sibling], slot + 2)
        else:
            far = int(event == "d")
            forward(2, far, 0, [sibling], slot)
            forward(2, far, 1, [sibling], slot + 1)

    def x_copy(s, src, dst, h):
        return pltpu.make_async_remote_copy(
            src_ref=src,
            dst_ref=dst,
            send_sem=x_ss.at[s, h],
            recv_sem=x_rs.at[s, xh],
            device_id=side[h],
            device_id_type=MESH,
        )

    def z_copy(s, src, dst):
        return pltpu.make_async_remote_copy(
            src_ref=src,
            dst_ref=dst,
            send_sem=z_ss.at[s],
            recv_sem=z_rs.at[s],
            device_id=znear,
            device_id_type=MESH,
        )

    def arrived(ref, sem):
        pltpu.make_async_copy(ref, ref, sem).wait()

    def out_rows(tt):
        return pl.ds(pl.multiple_of(lax.rem(tt, 8) * ROWS, ROWS), ROWS)

    def out_copy(s, tt):
        rows = out_rows(tt)
        return pltpu.make_async_copy(out.at[rows], out_h.at[rows], o_sem.at[s])

    def reader(slot, b):
        return lambda col: acc[slot, block_rows(b), cols(col)]

    def add(slot, b, *tiles):
        rows = block_rows(b)
        for col in range(TILES):
            total = acc[slot, rows, cols(col)]
            for tile in tiles:
                total = total + tile(col)
            acc[slot, rows, cols(col)] = total

    def finish(s, slot, tt, *tiles):
        rows = out_rows(tt)
        for col in range(TILES):
            total = acc[slot, block_rows(2 * zl + xh), cols(col)]
            for tile in tiles:
                total = total + tile(col)
            out[rows, cols(col)] = total * (1.0 / 8192)
        out_copy(s, tt).start()

    def x_op1(s, slot, tt, own):
        @pl.when(jnp.logical_not(own))
        def _():
            for h in range(2):
                arrived(xr.at[s, 2 * h], x_rs.at[s, h])
                add(slot, 2 * xh + 1 - h, decoder(xr.at[s, 2 * h]))
            for h in range(2):

                @pl.loop(0, 2)
                def _(zb):
                    encode(reader(slot, 2 * zb + h), xs.at[s, 2 * h + zb])

                x_copy(s, xs.at[s, pl.ds(2 * h, 2)], xr.at[s, pl.ds(2 * xh, 2)], h).start()

    def x_op2(s, slot, tt, own):
        @pl.when(own)
        def _():
            for h in range(2):
                arrived(xr.at[s, pl.ds(2 * h, 2)], x_rs.at[s, h])

            @pl.loop(0, 2)
            def _(i):
                zb = lax.rem(1 - zl + i, 2)
                add(slot, 2 * zb + xh, decoder(xr.at[s, zb]), decoder(xr.at[s, 2 + zb]))

                @pl.when(i == 0)
                def _():
                    encode(reader(slot, 2 * zb + xh), xs.at[s, 2])
                    z_copy(s, xs.at[s, 2], xr.at[s, 4]).start()

    def x_op3(s, slot, tt, own):
        @pl.when(own)
        def _():
            arrived(xr.at[s, 4], z_rs.at[s])
            finish(s, slot, tt, decoder(xr.at[s, 4]))

    def z_op1(s, slot, tt, own):
        arrived(xr.at[s, pl.ds(2, 2)], z_rs.at[s])

        @pl.loop(0, 2)
        def _(h):
            add(slot, 2 * zl + h, decoder(xr.at[s, 2 + h]))

        @pl.when(own)
        def _():
            for h in range(2):
                tiles = tuple(range(h * TILES // 2, (h + 1) * TILES // 2))
                encode(reader(slot, 2 * zl + 1 - xh), xs.at[s, h], tiles)
                part = pl.ds(0, HALF_UNIT)
                x_copy(s, xs.at[s, h, part], xr.at[s, xh, part], h).start()

    def z_op2(s, slot, tt, own):
        @pl.when(jnp.logical_not(own))
        def _():
            for h in range(2):
                arrived(xr.at[s, h, pl.ds(0, HALF_UNIT)], x_rs.at[s, h])
                tile = decoder(xr.at[s, h], TILES // 2)
                rows = block_rows(2 * zl + 1 - h)
                for at in range(TILES // 2):
                    lanes = pl.ds(pl.multiple_of((xh * (TILES // 2) + at) * LANES, LANES), LANES)
                    acc[slot, rows, lanes] += tile(at)
            for h in range(2):
                encode(reader(slot, 2 * zl + h), xs.at[s, h])
                x_copy(s, xs.at[s, h], xr.at[s, xh], h).start()

    def z_op3(s, slot, tt, own):
        @pl.when(own)
        def _():
            for h in range(2):
                arrived(xr.at[s, h], x_rs.at[s, h])
            finish(s, slot, tt, decoder(xr.at[s, 0]), decoder(xr.at[s, 1]))

    later = {("X", 1): x_op1, ("X", 2): x_op2, ("X", 3): x_op3, ("Z", 1): z_op1, ("Z", 2): z_op2, ("Z", 3): z_op3}

    def run_later(step, op):
        for mode in ("X", "Z"):
            lag = LAGS[mode, op]
            s = jnp.clip(step - lag, 0, SLICES - 1)
            tt, own, zfirst = slice_at(s)
            live = (step >= lag) & (step < SLICES + lag) & (zfirst == int(mode == "Z"))

            @pl.when(live)
            def _():
                later[mode, op](s, lax.rem(s, FSLOTS), tt, own)

    def run_first(step):
        @pl.when(step < SLICES)
        def _():
            s = jnp.minimum(step, SLICES - 1)
            slot = lax.rem(s, FSLOTS)
            tt, own, zfirst = slice_at(s)

            @pl.when(lax.rem(pick(s, codes) // 8, 2) == 1)
            def _():
                a_wait(tt, 0)
                a_wait(tt, 1)

            acc[slot] = jnp.dot(s_in[tt], s_out[...], preferred_element_type=F32)

            @pl.when((zfirst == 0) & own)
            def _():
                for zb in range(2):
                    encode(reader(slot, 2 * zb + 1 - xh), xs.at[s, zb])
                    x_copy(s, xs.at[s, zb], xr.at[s, 2 * xh], zb).start()

            @pl.when(zfirst == 1)
            def _():
                @pl.loop(0, 2)
                def _(h):
                    encode(reader(slot, 2 * (1 - zl) + h), xs.at[s, 2 + h])

                z_copy(s, xs.at[s, pl.ds(2, 2)], xr.at[s, pl.ds(2, 2)]).start()

    @pl.loop(0, LAST)
    def _(step):
        for part in SEQUENCE:
            if part == 0:
                run_first(step)
            elif part == "ev":
                for event, when in EVENTS:

                    @pl.when(step == when)
                    def _():
                        gather(event)
            else:
                run_later(step, part)

    @pl.loop(0, 28)
    def _(at):
        arrived(half_of(t, 0), a_ss.at[at])

    for half in range(2):
        arrived(ib.at[pl.ds(2 * half, 2)], b_ss.at[half])

    @pl.loop(0, SLICES)
    def _(s):
        tt, own, zfirst = slice_at(s)
        for mode in range(2):
            for role in range(2):

                @pl.when((zfirst == mode) & (own == (role == 1)))
                def _():
                    if mode == 0:
                        ref = xs.at[s, pl.ds(0, 1 if role else 2)]
                    else:
                        ref = xs.at[s, 0, pl.ds(0, HALF_UNIT)] if role else xs.at[s, 0]
                    for h in range(2):
                        arrived(ref, x_ss.at[s, h])
                    if mode or role:
                        arrived(xs.at[s, pl.ds(2, 1 + mode)], z_ss.at[s])
                    if role:
                        out_copy(s, tt).wait()


def per_device(activations, out_grads, input_basis, output_basis):
    any_spec = pl.BlockSpec(memory_space=pl.ANY)
    dma = pltpu.SemaphoreType.DMA
    return pl.pallas_call(
        kernel,
        out_shape=jax.ShapeDtypeStruct((8 * ROWS, WIDTH), F32),
        in_specs=[any_spec] * 4,
        out_specs=any_spec,
        scratch_shapes=[
            pltpu.VMEM((NBLK, 1024, WIDTH), BF16),
            pltpu.VMEM((1024, WIDTH), BF16),
            pltpu.VMEM((NBLK, ROWS, WIDTH), BF16),
            pltpu.VMEM((NBLK, ROWS, WIDTH), BF16),
            pltpu.VMEM((1024, WIDTH), BF16),
            pltpu.VMEM((SLICES, NBLK * ROWS, 1024), BF16),
            pltpu.VMEM((1024, WIDTH), BF16),
            pltpu.VMEM((FSLOTS, NBLK * ROWS, WIDTH), F32),
            pltpu.VMEM((SLICES, 4, UNIT, LANES), BF16),
            pltpu.VMEM((SLICES, 5, UNIT, LANES), BF16),
            pltpu.VMEM((8 * ROWS, WIDTH), F32),
            dma((7,)),
            dma((2,)),
            dma((2,)),
            dma((28,)),
            dma((SLICES, 2)),
            dma((SLICES, 2)),
            dma((SLICES, 2)),
            dma((SLICES,)),
            dma((SLICES,)),
            dma((SLICES,)),
        ],
        compiler_params=pltpu.CompilerParams(
            collective_id=0, has_side_effects=True, vmem_limit_bytes=60 * 2**20
        ),
        cost_estimate=pl.CostEstimate(
            flops=12 * 10**9, bytes_accessed=16 * 2**20, transcendentals=10**7
        ),
        name="scaling",
    )(activations, out_grads, input_basis, output_basis)


def solution(mesh):
    return jax.shard_map(
        per_device,
        mesh=mesh,
        in_specs=(
            P("dp", None),
            P("dp", "tensor"),
            P(None, "tensor", None),
            P("tensor", None, None),
        ),
        out_specs=P("dp", "tensor"),
        check_vma=False,
    )
```

time: 122 us -> 91.9 us (0.75)
  the two profiles are of different devices: /device:TPU:6 before, /device:TPU:0 now
where the time goes in v2:
time: 91.9 us; the launch traced here: 91.8 us
  Pallas kernels  88.6 us (96%)
  local copies, waits for them, and re-layouts  3.16 us (3%)
    pallas_call x1, Pallas kernels, per_device(): pl.pallas_call(kernel, out_shape=jax.ShapeDtypeStruct((8 * ROWS, WIDTH),...  88.6 us
    unnamed x1, local copies, waits for them, and re-layouts  3.16 us

profile of v2, /device:TPU:0, one launch (start us, length us, event | category | flops | bytes accessed | tf_op | source)
XLA Modules:
  0.0 91.8 jit_solution(16297819173062203442)
XLA Ops:
  0.0 88.6 %scaling.1 = f32[512,1024]{1,0:T(8,128)} custom-call(bf16[1024,4096]{1,0:T(8,128)(2,1)} %act_h.1, bf16[1024,1024]{1,0:T(8,128)(2,1)} %grad_h.1, bf16[4,64,1024]{2,1,0:T(8,128)(2,1)} %ib_h.1, bf16[1,1024,1024]{2,1,0:T(8,128)(2,1)} %ob_h.1), custom_call_target="tpu_custom_call" | custom-call | flops 12000000000 | bytes 16777216 | tf_op jit(solution)/shard_map/scaling/pallas_call | solution.py:446
  88.6 3.2 %copy.6 = f32[512,1024]{1,0:T(8,128)} copy(f32[512,1024]{1,0:T(8,128)} %scaling.1) | data formatting | bytes 4194304

commit v3 on v2

--- a/solution.py
+++ b/solution.py
@@ -17,35 +17,35 @@
 UNIT = TILES * ROWS + 16
 HALF_UNIT = TILES // 2 * ROWS + 16
 SLICES = 16
-FSLOTS = 9
+FSLOTS = 12
 ORDER = [
-    (0, 0, 1, 1),
-    (0, 0, 0, 0),
+    (0, 0, 1, 0),
+    (0, 0, 0, 1),
     (3, 0, 0, 0),
+    (3, 0, 1, 1),
+    (1, 0, 1, 0),
+    (2, 0, 0, 0),
     (1, 0, 0, 1),
-    (1, 0, 1, 1),
-    (3, 0, 1, 0),
     (0, 1, 0, 0),
-    (2, 0, 0, 0),
-    (2, 0, 1, 1),
-    (0, 1, 1, 0),
+    (2, 0, 1, 0),
+    (0, 1, 1, 1),
+    (3, 1, 0, 0),
     (3, 1, 1, 1),
-    (3, 1, 0, 0),
     (1, 1, 1, 0),
-    (2, 1, 1, 1),
-    (2, 1, 0, 0),
     (1, 1, 0, 1),
+    (2, 1, 1, 0),
+    (2, 1, 0, 1),
 ]
 LAGS = {
-    ("X", 1): 2,
+    ("X", 1): 3,
     ("X", 2): 7,
-    ("X", 3): 8,
+    ("X", 3): 10,
     ("Z", 1): 3,
-    ("Z", 2): 6,
-    ("Z", 3): 8,
+    ("Z", 2): 7,
+    ("Z", 3): 11,
 }
-EVENTS = [("a0", 2), ("a1", 2), ("z0", 1), ("z1", 6), ("b0", 8), ("b1", 8), ("c", 7), ("d", 12)]
-SEQUENCE = (2, "ev", 0, 1, 3)
+EVENTS = [("a0", 1), ("a1", 2), ("z0", 3), ("z1", 5), ("b0", 9), ("b1", 10), ("c", 5), ("d", 13)]
+SEQUENCE = ("ev", 0, 1, 2, 3)
 SLOTS = {"z0": 6, "z1": 9, "a0": 12, "a1": 15, "b0": 18, "b1": 21, "c": 24, "d": 26}
 LAST = SLICES + max(LAGS.values())
 TINY = float(2.0**-100)
@@ -100,9 +100,9 @@
 
 
 def kernel(
-    act_h, grad_h, ib_h, ob_h, out_h,
-    act, grad, ib, ib_far, ob, s_in, s_out, acc, xs, xr, out,
-    ld_sem, b_ss, b_rs, a_ss, a_rs, x_ss, x_rs, z_ss, z_rs, o_sem,
+    act_h, grad_h, ib_h, ob_h, out,
+    act, grad, ib, ib_far, ob, s_in, s_out, acc, xs, xr,
+    ld_sem, b_ss, b_rs, a_ss, a_rs, x_ss, x_rs, z_ss, z_rs,
 ):
     dp, t = lax.axis_index("dp"), lax.axis_index("tensor")
     x, zl = lax.rem(dp, 4), dp // 4
@@ -161,35 +161,27 @@
         )
 
     def rotate(basis, b, tt):
-        @pl.loop(0, 2)
-        def _(j):
-            part = pl.ds(pl.multiple_of(j * 512, 512), 512)
-            turned = lax.dot_general(
-                basis[b], act[b, part, :], (((1,), (1,)), ((), ())), preferred_element_type=F32
-            )
-            s_in[tt, block_rows(b), part] = (turned * turned).astype(BF16)
+        turned = lax.dot_general(
+            basis[b], act[b], (((1,), (1,)), ((), ())), preferred_element_type=F32
+        )
+        s_in[tt, block_rows(b), :] = (turned * turned).astype(BF16)
 
     loads[0].wait()
     for b in range(NBLK):
         loads[1 + b].wait()
         rotate(ib, b, t)
-        if b == 0:
-            pl.semaphore_wait(barrier, len(partners))
-        if b % 2 == 1:
-            half = b // 2
-            for at, target in enumerate((y3, y1, sibling)):
-                a_copy(t, half, target, half * 3 + at).start()
-            b_copy(half).start()
+    pl.semaphore_wait(barrier, len(partners))
+    for half in range(2):
+        for at, target in enumerate((y3, y1, sibling)):
+            a_copy(t, half, target, half * 3 + at).start()
+        b_copy(half).start()
     loads[5].wait()
     loads[6].wait()
 
-    @pl.loop(0, 4)
-    def _(j):
-        part = pl.ds(pl.multiple_of(j * 256, 256), 256)
-        turned = lax.dot_general(
-            grad[...], ob[part, :], (((1,), (1,)), ((), ())), preferred_element_type=F32
-        )
-        s_out[:, part] = (turned * turned).astype(BF16)
+    turned = lax.dot_general(
+        grad[...], ob[...], (((1,), (1,)), ((), ())), preferred_element_type=F32
+    )
+    s_out[...] = (turned * turned).astype(BF16)
 
     codes = [e + 4 * far + 8 * other + 16 * zfirst for e, far, other, zfirst in ORDER]
 
@@ -262,10 +254,6 @@
     def out_rows(tt):
         return pl.ds(pl.multiple_of(lax.rem(tt, 8) * ROWS, ROWS), ROWS)
 
-    def out_copy(s, tt):
-        rows = out_rows(tt)
-        return pltpu.make_async_copy(out.at[rows], out_h.at[rows], o_sem.at[s])
-
     def reader(slot, b):
         return lambda col: acc[slot, block_rows(b), cols(col)]
 
@@ -284,7 +272,6 @@
             for tile in tiles:
                 total = total + tile(col)
             out[rows, cols(col)] = total * (1.0 / 8192)
-        out_copy(s, tt).start()
 
     def x_op1(s, slot, tt, own):
         @pl.when(jnp.logical_not(own))
@@ -436,8 +423,6 @@
                         arrived(ref, x_ss.at[s, h])
                     if mode or role:
                         arrived(xs.at[s, pl.ds(2, 1 + mode)], z_ss.at[s])
-                    if role:
-                        out_copy(s, tt).wait()
 
 
 def per_device(activations, out_grads, input_basis, output_basis):
@@ -445,9 +430,9 @@
     dma = pltpu.SemaphoreType.DMA
     return pl.pallas_call(
         kernel,
-        out_shape=jax.ShapeDtypeStruct((8 * ROWS, WIDTH), F32),
+        out_shape=pltpu.VMEM((8 * ROWS, WIDTH), F32),
         in_specs=[any_spec] * 4,
-        out_specs=any_spec,
+        out_specs=pl.BlockSpec(memory_space=pltpu.VMEM),
         scratch_shapes=[
             pltpu.VMEM((NBLK, 1024, WIDTH), BF16),
             pltpu.VMEM((1024, WIDTH), BF16),
@@ -459,7 +444,6 @@
             pltpu.VMEM((FSLOTS, NBLK * ROWS, WIDTH), F32),
             pltpu.VMEM((SLICES, 4, UNIT, LANES), BF16),
             pltpu.VMEM((SLICES, 5, UNIT, LANES), BF16),
-            pltpu.VMEM((8 * ROWS, WIDTH), F32),
             dma((7,)),
             dma((2,)),
             dma((2,)),
@@ -469,10 +453,9 @@
             dma((SLICES, 2)),
             dma((SLICES,)),
             dma((SLICES,)),
-            dma((SLICES,)),
         ],
         compiler_params=pltpu.CompilerParams(
-            collective_id=0, has_side_effects=True, vmem_limit_bytes=60 * 2**20
+            collective_id=0, has_side_effects=True, vmem_limit_bytes=57 * 2**20
         ),
         cost_estimate=pl.CostEstimate(
             flops=12 * 10**9, bytes_accessed=16 * 2**20, transcendentals=10**7

time: 91.9 us -> 84.3 us (0.917); the launches traced: 91.8 us -> 83.1 us
  Pallas kernels: 88.6 us -> 81.8 us
  local copies, waits for them, and re-layouts: 3.16 us -> 1.32 us
    pallas_call x1, Pallas kernels: 88.6 us -> 81.8 us  [per_device(): pl.pallas_call(kernel, out_shape=pltpu.VMEM((8 * ROWS, WIDTH), F32), in_s...]
    unnamed x1, local copies, waits for them, and re-layouts: 3.16 us -> 1.32 us
where the time goes in v3:
time: 84.3 us; the launch traced here: 83.1 us
  Pallas kernels  81.8 us (97%)
  local copies, waits for them, and re-layouts  1.32 us (2%)
    pallas_call x1, Pallas kernels, per_device(): pl.pallas_call(kernel, out_shape=pltpu.VMEM((8 * ROWS, WIDTH), F32), in_s...  81.8 us

profile of v3, /device:TPU:0, one launch (start us, length us, event | category | flops | bytes accessed | tf_op | source)
XLA Modules:
  0.0 83.1 jit_solution(17696377546279569257)
XLA Ops:
  0.0 81.8 %scaling.1 = f32[512,1024]{1,0:T(8,128)S(1)} custom-call(bf16[1024,4096]{1,0:T(8,128)(2,1)} %act_h.1, bf16[1024,1024]{1,0:T(8,128)(2,1)} %grad_h.1, bf16[4,64,1024]{2,1,0:T(8,128)(2,1)} %ib_h.1, bf16[1,1024,1024]{2,1,0:T(8,128)(2,1)} %ob_h.1), custom_call_target="tpu_custom_call" | custom-call | flops 12000000000 | bytes 16777216 | tf_op jit(solution)/shard_map/scaling/pallas_call | solution.py:431
  81.8 1.3 %copy.6 = f32[512,1024]{1,0:T(8,128)} copy(f32[512,1024]{1,0:T(8,128)S(1)} %scaling.1) | data formatting | bytes 4194304

commit v4 on v3

--- a/solution.py
+++ b/solution.py
@@ -19,33 +19,33 @@
 SLICES = 16
 FSLOTS = 12
 ORDER = [
+    (0, 0, 0, 1),
     (0, 0, 1, 0),
-    (0, 0, 0, 1),
     (3, 0, 0, 0),
-    (3, 0, 1, 1),
+    (1, 0, 0, 1),
     (1, 0, 1, 0),
-    (2, 0, 0, 0),
-    (1, 0, 0, 1),
-    (0, 1, 0, 0),
+    (3, 0, 1, 0),
+    (2, 0, 0, 1),
     (2, 0, 1, 0),
     (0, 1, 1, 1),
+    (0, 1, 0, 0),
     (3, 1, 0, 0),
     (3, 1, 1, 1),
-    (1, 1, 1, 0),
-    (1, 1, 0, 1),
-    (2, 1, 1, 0),
-    (2, 1, 0, 1),
+    (1, 1, 0, 0),
+    (2, 1, 0, 0),
+    (1, 1, 1, 1),
+    (2, 1, 1, 1),
 ]
 LAGS = {
-    ("X", 1): 3,
-    ("X", 2): 7,
-    ("X", 3): 10,
+    ("X", 1): 2,
+    ("X", 2): 6,
+    ("X", 3): 9,
     ("Z", 1): 3,
     ("Z", 2): 7,
     ("Z", 3): 11,
 }
-EVENTS = [("a0", 1), ("a1", 2), ("z0", 3), ("z1", 5), ("b0", 9), ("b1", 10), ("c", 5), ("d", 13)]
-SEQUENCE = ("ev", 0, 1, 2, 3)
+EVENTS = [("a0", 2), ("a1", 2), ("z0", 4), ("z1", 5), ("b0", 8), ("b1", 9), ("c", 5), ("d", 12)]
+SEQUENCE = ("ev", 0, 2, 1, 3)
 SLOTS = {"z0": 6, "z1": 9, "a0": 12, "a1": 15, "b0": 18, "b1": 21, "c": 24, "d": 26}
 LAST = SLICES + max(LAGS.values())
 TINY = float(2.0**-100)
@@ -170,11 +170,14 @@
     for b in range(NBLK):
         loads[1 + b].wait()
         rotate(ib, b, t)
-    pl.semaphore_wait(barrier, len(partners))
-    for half in range(2):
-        for at, target in enumerate((y3, y1, sibling)):
-            a_copy(t, half, target, half * 3 + at).start()
-        b_copy(half).start()
+        if b % 2 == 1:
+            half = b // 2
+            if half == 0:
+                pl.semaphore_wait(barrier, len(partners))
+                b_copy(0).start()
+                b_copy(1).start()
+            for at, target in enumerate((y3, y1, sibling)):
+                a_copy(t, half, target, half * 3 + at).start()
     loads[5].wait()
     loads[6].wait()
 

time: 84.3 us -> 82.7 us (0.981); the launches traced: 83.1 us -> 82.6 us
  no operation moved by 1% of the time
where the time goes in v4:
time: 82.7 us; the launch traced here: 82.6 us
  Pallas kernels  81.3 us (98%)
  local copies, waits for them, and re-layouts  1.32 us (2%)
    pallas_call x1, Pallas kernels, per_device(): pl.pallas_call(kernel, out_shape=pltpu.VMEM((8 * ROWS, WIDTH), F32), in_s...  81.3 us

profile of v4, /device:TPU:0, one launch (start us, length us, event | category | flops | bytes accessed | tf_op | source)
XLA Modules:
  0.0 82.6 jit_solution(1192555599140277475)
XLA Ops:
  0.0 81.3 %scaling.1 = f32[512,1024]{1,0:T(8,128)S(1)} custom-call(bf16[1024,4096]{1,0:T(8,128)(2,1)} %act_h.1, bf16[1024,1024]{1,0:T(8,128)(2,1)} %grad_h.1, bf16[4,64,1024]{2,1,0:T(8,128)(2,1)} %ib_h.1, bf16[1,1024,1024]{2,1,0:T(8,128)(2,1)} %ob_h.1), custom_call_target="tpu_custom_call" | custom-call | flops 12000000000 | bytes 16777216 | tf_op jit(solution)/shard_map/scaling/pallas_call | solution.py:434
  81.3 1.3 %copy.6 = f32[512,1024]{1,0:T(8,128)} copy(f32[512,1024]{1,0:T(8,128)S(1)} %scaling.1) | data formatting | bytes 4194304

commit v5 on v4

--- a/solution.py
+++ b/solution.py
@@ -16,6 +16,8 @@
 TILES = WIDTH // LANES
 UNIT = TILES * ROWS + 16
 HALF_UNIT = TILES // 2 * ROWS + 16
+DATA = TILES * ROWS
+PAIR = 2 * DATA + 16
 SLICES = 16
 FSLOTS = 12
 ORDER = [
@@ -44,7 +46,7 @@
     ("Z", 2): 7,
     ("Z", 3): 11,
 }
-EVENTS = [("a0", 2), ("a1", 2), ("z0", 4), ("z1", 5), ("b0", 8), ("b1", 9), ("c", 5), ("d", 12)]
+EVENTS = [("a0", 1), ("a1", 2), ("z0", 4), ("z1", 5), ("b0", 9), ("b1", 9), ("d", 12), ("c", 5)]
 SEQUENCE = ("ev", 0, 2, 1, 3)
 SLOTS = {"z0": 6, "z1": 9, "a0": 12, "a1": 15, "b0": 18, "b1": 21, "c": 24, "d": 26}
 LAST = SLICES + max(LAGS.values())
@@ -64,26 +66,34 @@
     return lax.rem(y + e, 2) + 2 * lax.rem(y // 2 + e // 2, 2)
 
 
-def encode(read, unit, tiles=tuple(range(TILES))):
-    top = read(tiles[0]).reshape(ROWS // 8, 8, LANES).max(axis=0)
-    for col in tiles[1:]:
-        top = jnp.maximum(top, read(col).reshape(ROWS // 8, 8, LANES).max(axis=0))
+def rows_of(start, count):
+    return pl.ds(pl.multiple_of(start, 16), count)
+
+
+def encode(reads, buf, s, row, tiles=tuple(range(TILES))):
+    top = None
+    for read in reads:
+        for col in tiles:
+            high = read(col).reshape(ROWS // 8, 8, LANES).max(axis=0)
+            top = high if top is None else jnp.maximum(top, high)
     scale = jnp.maximum(top, TINY).astype(BF16).astype(F32)
     inv = UP / scale
-    unit[pl.ds(len(tiles) * ROWS, 16), :] = jnp.concatenate([scale, scale], axis=0).astype(BF16)
-    for at, col in enumerate(tiles):
-        v = (read(col).reshape(ROWS // 8, 8, LANES) * inv).reshape(ROWS, LANES)
-        v = v * v
-        v = v * v
-        v = v * v
-        unit[pl.ds(at * ROWS, ROWS), :] = v.astype(BF16)
-
-
-def decoder(unit, tiles=TILES):
-    scale = unit[pl.ds(tiles * ROWS, 16), :].astype(F32)[0:8] * (1.0 / UP)
+    for read in reads:
+        for col in tiles:
+            v = (read(col).reshape(ROWS // 8, 8, LANES) * inv).reshape(ROWS, LANES)
+            v = v * v
+            v = v * v
+            v = v * v
+            buf[s, rows_of(row, ROWS), :] = v.astype(BF16)
+            row = row + ROWS
+    buf[s, rows_of(row, 16), :] = jnp.concatenate([scale, scale], axis=0).astype(BF16)
+
+
+def decoder(buf, s, row, scale_row):
+    scale = buf[s, rows_of(scale_row, 16), :].astype(F32)[0:8] * (1.0 / UP)
 
     def tile(col):
-        v = jnp.maximum(unit[pl.ds(col * ROWS, ROWS), :].astype(F32), FLOOR)
+        v = jnp.maximum(buf[s, rows_of(row + col * ROWS, ROWS), :].astype(F32), FLOOR)
         w = lax.rsqrt(lax.rsqrt(v))
         v = w * lax.rsqrt(w)
         return (v.reshape(ROWS // 8, 8, LANES) * scale).reshape(ROWS, LANES)
@@ -231,6 +241,9 @@
             forward(2, far, 0, [sibling], slot)
             forward(2, far, 1, [sibling], slot + 1)
 
+    def part(buf, s, row, count):
+        return buf.at[s, rows_of(row, count)]
+
     def x_copy(s, src, dst, h):
         return pltpu.make_async_remote_copy(
             src_ref=src,
@@ -280,73 +293,74 @@
         @pl.when(jnp.logical_not(own))
         def _():
             for h in range(2):
-                arrived(xr.at[s, 2 * h], x_rs.at[s, h])
-                add(slot, 2 * xh + 1 - h, decoder(xr.at[s, 2 * h]))
-            for h in range(2):
-
-                @pl.loop(0, 2)
-                def _(zb):
-                    encode(reader(slot, 2 * zb + h), xs.at[s, 2 * h + zb])
-
-                x_copy(s, xs.at[s, pl.ds(2 * h, 2)], xr.at[s, pl.ds(2 * xh, 2)], h).start()
+                row = 2 * h * UNIT
+                arrived(part(xr, s, row, UNIT), x_rs.at[s, h])
+                add(slot, 2 * xh + 1 - h, decoder(xr, s, row, row + DATA))
+            for h in range(2):
+                row = 2 * h * UNIT
+                encode([reader(slot, h), reader(slot, 2 + h)], xs, s, row)
+                x_copy(s, part(xs, s, row, PAIR), part(xr, s, 2 * xh * UNIT, PAIR), h).start()
 
     def x_op2(s, slot, tt, own):
         @pl.when(own)
         def _():
             for h in range(2):
-                arrived(xr.at[s, pl.ds(2 * h, 2)], x_rs.at[s, h])
+                arrived(part(xr, s, 2 * h * UNIT, PAIR), x_rs.at[s, h])
 
             @pl.loop(0, 2)
             def _(i):
                 zb = lax.rem(1 - zl + i, 2)
-                add(slot, 2 * zb + xh, decoder(xr.at[s, zb]), decoder(xr.at[s, 2 + zb]))
+                tiles = [
+                    decoder(xr, s, row + zb * DATA, row + 2 * DATA) for row in (0, 2 * UNIT)
+                ]
+                add(slot, 2 * zb + xh, *tiles)
 
                 @pl.when(i == 0)
                 def _():
-                    encode(reader(slot, 2 * zb + xh), xs.at[s, 2])
-                    z_copy(s, xs.at[s, 2], xr.at[s, 4]).start()
+                    encode([reader(slot, 2 * zb + xh)], xs, s, 2 * UNIT)
+                    z_copy(s, part(xs, s, 2 * UNIT, UNIT), part(xr, s, 4 * UNIT, UNIT)).start()
 
     def x_op3(s, slot, tt, own):
         @pl.when(own)
         def _():
-            arrived(xr.at[s, 4], z_rs.at[s])
-            finish(s, slot, tt, decoder(xr.at[s, 4]))
+            arrived(part(xr, s, 4 * UNIT, UNIT), z_rs.at[s])
+            finish(s, slot, tt, decoder(xr, s, 4 * UNIT, 4 * UNIT + DATA))
 
     def z_op1(s, slot, tt, own):
-        arrived(xr.at[s, pl.ds(2, 2)], z_rs.at[s])
+        arrived(part(xr, s, 2 * UNIT, PAIR), z_rs.at[s])
 
         @pl.loop(0, 2)
         def _(h):
-            add(slot, 2 * zl + h, decoder(xr.at[s, 2 + h]))
+            add(slot, 2 * zl + h, decoder(xr, s, 2 * UNIT + h * DATA, 2 * UNIT + 2 * DATA))
 
         @pl.when(own)
         def _():
             for h in range(2):
                 tiles = tuple(range(h * TILES // 2, (h + 1) * TILES // 2))
-                encode(reader(slot, 2 * zl + 1 - xh), xs.at[s, h], tiles)
-                part = pl.ds(0, HALF_UNIT)
-                x_copy(s, xs.at[s, h, part], xr.at[s, xh, part], h).start()
+                encode([reader(slot, 2 * zl + 1 - xh)], xs, s, h * UNIT, tiles)
+                src, dst = part(xs, s, h * UNIT, HALF_UNIT), part(xr, s, xh * UNIT, HALF_UNIT)
+                x_copy(s, src, dst, h).start()
 
     def z_op2(s, slot, tt, own):
         @pl.when(jnp.logical_not(own))
         def _():
             for h in range(2):
-                arrived(xr.at[s, h, pl.ds(0, HALF_UNIT)], x_rs.at[s, h])
-                tile = decoder(xr.at[s, h], TILES // 2)
+                arrived(part(xr, s, h * UNIT, HALF_UNIT), x_rs.at[s, h])
+                tile = decoder(xr, s, h * UNIT, h * UNIT + HALF_UNIT - 16)
                 rows = block_rows(2 * zl + 1 - h)
                 for at in range(TILES // 2):
                     lanes = pl.ds(pl.multiple_of((xh * (TILES // 2) + at) * LANES, LANES), LANES)
                     acc[slot, rows, lanes] += tile(at)
             for h in range(2):
-                encode(reader(slot, 2 * zl + h), xs.at[s, h])
-                x_copy(s, xs.at[s, h], xr.at[s, xh], h).start()
+                encode([reader(slot, 2 * zl + h)], xs, s, h * UNIT)
+                x_copy(s, part(xs, s, h * UNIT, UNIT), part(xr, s, xh * UNIT, UNIT), h).start()
 
     def z_op3(s, slot, tt, own):
         @pl.when(own)
         def _():
             for h in range(2):
-                arrived(xr.at[s, h], x_rs.at[s, h])
-            finish(s, slot, tt, decoder(xr.at[s, 0]), decoder(xr.at[s, 1]))
+                arrived(part(xr, s, h * UNIT, UNIT), x_rs.at[s, h])
+            finish(s, slot, tt, decoder(xr, s, 0, DATA), decoder(xr, s, UNIT, UNIT + DATA))
 
     later = {("X", 1): x_op1, ("X", 2): x_op2, ("X", 3): x_op3, ("Z", 1): z_op1, ("Z", 2): z_op2, ("Z", 3): z_op3}
 
@@ -378,16 +392,15 @@
             @pl.when((zfirst == 0) & own)
             def _():
                 for zb in range(2):
-                    encode(reader(slot, 2 * zb + 1 - xh), xs.at[s, zb])
-                    x_copy(s, xs.at[s, zb], xr.at[s, 2 * xh], zb).start()
+                    encode([reader(slot, 2 * zb + 1 - xh)], xs, s, zb * UNIT)
+                    src, dst = part(xs, s, zb * UNIT, UNIT), part(xr, s, 2 * xh * UNIT, UNIT)
+                    x_copy(s, src, dst, zb).start()
 
             @pl.when(zfirst == 1)
             def _():
-                @pl.loop(0, 2)
-                def _(h):
-                    encode(reader(slot, 2 * (1 - zl) + h), xs.at[s, 2 + h])
-
-                z_copy(s, xs.at[s, pl.ds(2, 2)], xr.at[s, pl.ds(2, 2)]).start()
+                reads = [reader(slot, 2 * (1 - zl) + h) for h in range(2)]
+                encode(reads, xs, s, 2 * UNIT)
+                z_copy(s, part(xs, s, 2 * UNIT, PAIR), part(xr, s, 2 * UNIT, PAIR)).start()
 
     @pl.loop(0, LAST)
     def _(step):
@@ -418,14 +431,11 @@
 
                 @pl.when((zfirst == mode) & (own == (role == 1)))
                 def _():
-                    if mode == 0:
-                        ref = xs.at[s, pl.ds(0, 1 if role else 2)]
-                    else:
-                        ref = xs.at[s, 0, pl.ds(0, HALF_UNIT)] if role else xs.at[s, 0]
+                    count = ((PAIR, UNIT), (UNIT, HALF_UNIT))[mode][role]
                     for h in range(2):
-                        arrived(ref, x_ss.at[s, h])
+                        arrived(part(xs, s, 0, count), x_ss.at[s, h])
                     if mode or role:
-                        arrived(xs.at[s, pl.ds(2, 1 + mode)], z_ss.at[s])
+                        arrived(part(xs, s, 2 * UNIT, PAIR if mode else UNIT), z_ss.at[s])
 
 
 def per_device(activations, out_grads, input_basis, output_basis):
@@ -445,8 +455,8 @@
             pltpu.VMEM((SLICES, NBLK * ROWS, 1024), BF16),
             pltpu.VMEM((1024, WIDTH), BF16),
             pltpu.VMEM((FSLOTS, NBLK * ROWS, WIDTH), F32),
-            pltpu.VMEM((SLICES, 4, UNIT, LANES), BF16),
-            pltpu.VMEM((SLICES, 5, UNIT, LANES), BF16),
+            pltpu.VMEM((SLICES, 4 * UNIT, LANES), BF16),
+            pltpu.VMEM((SLICES, 5 * UNIT, LANES), BF16),
             dma((7,)),
             dma((2,)),
             dma((2,)),

time: 82.7 us -> 82.1 us (level)
  no operation moved by 1% of the time
where the time goes in v5:
time: 82.1 us; the launch traced here: 82 us
  Pallas kernels  80.6 us (98%)
  local copies, waits for them, and re-layouts  1.32 us (2%)
    pallas_call x1, Pallas kernels, per_device(): pl.pallas_call(kernel, out_shape=pltpu.VMEM((8 * ROWS, WIDTH), F32), in_s...  80.6 us

profile of v5, /device:TPU:0, one launch (start us, length us, event | category | flops | bytes accessed | tf_op | source)
XLA Modules:
  0.0 82.0 jit_solution(10054860926822391213)
XLA Ops:
  0.0 80.6 %scaling.1 = f32[512,1024]{1,0:T(8,128)S(1)} custom-call(bf16[1024,4096]{1,0:T(8,128)(2,1)} %act_h.1, bf16[1024,1024]{1,0:T(8,128)(2,1)} %grad_h.1, bf16[4,64,1024]{2,1,0:T(8,128)(2,1)} %ib_h.1, bf16[1,1024,1024]{2,1,0:T(8,128)(2,1)} %ob_h.1), custom_call_target="tpu_custom_call" | custom-call | flops 12000000000 | bytes 16777216 | tf_op jit(solution)/shard_map/scaling/pallas_call | solution.py:444
  80.6 1.3 %copy.6 = f32[512,1024]{1,0:T(8,128)} copy(f32[512,1024]{1,0:T(8,128)S(1)} %scaling.1) | data formatting | bytes 4194304

commit v6 on v5

--- a/solution.py
+++ b/solution.py
@@ -20,35 +20,65 @@
 PAIR = 2 * DATA + 16
 SLICES = 16
 FSLOTS = 12
-ORDER = [
-    (0, 0, 0, 1),
-    (0, 0, 1, 0),
-    (3, 0, 0, 0),
-    (1, 0, 0, 1),
-    (1, 0, 1, 0),
-    (3, 0, 1, 0),
-    (2, 0, 0, 1),
-    (2, 0, 1, 0),
-    (0, 1, 1, 1),
-    (0, 1, 0, 0),
-    (3, 1, 0, 0),
-    (3, 1, 1, 1),
-    (1, 1, 0, 0),
-    (2, 1, 0, 0),
-    (1, 1, 1, 1),
-    (2, 1, 1, 1),
+ORDERS = [
+    [
+        (0, 0, 1, 1),
+        (0, 0, 0, 0),
+        (3, 0, 0, 0),
+        (1, 0, 1, 1),
+        (1, 0, 0, 0),
+        (3, 0, 1, 0),
+        (0, 1, 1, 1),
+        (2, 0, 0, 1),
+        (3, 1, 1, 0),
+        (0, 1, 0, 0),
+        (3, 1, 0, 0),
+        (2, 0, 1, 1),
+        (1, 1, 0, 1),
+        (1, 1, 1, 0),
+        (2, 1, 0, 0),
+        (2, 1, 1, 1),
+    ],
+    [
+        (0, 0, 0, 1),
+        (0, 0, 1, 0),
+        (3, 0, 1, 0),
+        (1, 0, 0, 1),
+        (1, 0, 1, 0),
+        (3, 0, 0, 0),
+        (0, 1, 0, 1),
+        (2, 0, 1, 1),
+        (3, 1, 0, 0),
+        (0, 1, 1, 0),
+        (3, 1, 1, 0),
+        (2, 0, 0, 1),
+        (1, 1, 1, 1),
+        (1, 1, 0, 0),
+        (2, 1, 1, 0),
+        (2, 1, 0, 1),
+    ],
 ]
 LAGS = {
     ("X", 1): 2,
-    ("X", 2): 6,
-    ("X", 3): 9,
+    ("X", 2): 5,
+    ("X", 3): 10,
     ("Z", 1): 3,
-    ("Z", 2): 7,
+    ("Z", 2): 6,
     ("Z", 3): 11,
 }
-EVENTS = [("a0", 1), ("a1", 2), ("z0", 4), ("z1", 5), ("b0", 9), ("b1", 9), ("d", 12), ("c", 5)]
-SEQUENCE = ("ev", 0, 2, 1, 3)
-SLOTS = {"z0": 6, "z1": 9, "a0": 12, "a1": 15, "b0": 18, "b1": 21, "c": 24, "d": 26}
+EVENTS = [
+    ("b1", (9, 11)),
+    ("d", (13, 13)),
+    ("a1", (3, 2)),
+    ("c", (6, 9)),
+    ("z0", (5, 2)),
+    ("b3", (8, 7)),
+    ("a3", (2, 4)),
+    ("z1", (5, 4)),
+]
+SEQUENCE = ("ev", 0, 1, 2, 3)
+SPLIT = True
+SLOTS = {"z0": 6, "z1": 9, "a3": 12, "a1": 15, "b3": 18, "b1": 21, "c": 24, "d": 26}
 LAST = SLICES + max(LAGS.values())
 TINY = float(2.0**-100)
 UP = float(2.0**14)
@@ -176,6 +206,13 @@
         )
         s_in[tt, block_rows(b), :] = (turned * turned).astype(BF16)
 
+    codes = []
+    for pair in zip(*ORDERS):
+        code0, code1 = (e + 4 * far + 8 * other + 16 * zfirst for e, far, other, zfirst in pair)
+        codes.append(code0 if code0 == code1 else jnp.where(core == 0, code0, code1))
+    y_first = dev(y=flip(y, jnp.where(core == 0, 3, 1))) if SPLIT else y3
+    y_second = dev(y=flip(y, jnp.where(core == 0, 1, 3))) if SPLIT else y1
+
     loads[0].wait()
     for b in range(NBLK):
         loads[1 + b].wait()
@@ -186,7 +223,7 @@
                 pl.semaphore_wait(barrier, len(partners))
                 b_copy(0).start()
                 b_copy(1).start()
-            for at, target in enumerate((y3, y1, sibling)):
+            for at, target in enumerate((y_first, sibling) if SPLIT else (y_first, sibling, y_second)):
                 a_copy(t, half, target, half * 3 + at).start()
     loads[5].wait()
     loads[6].wait()
@@ -196,7 +233,10 @@
     )
     s_out[...] = (turned * turned).astype(BF16)
 
-    codes = [e + 4 * far + 8 * other + 16 * zfirst for e, far, other, zfirst in ORDER]
+
+    if SPLIT:
+        for half in range(2):
+            a_copy(t, half, y_second, half * 3 + 2).start()
 
     def slice_at(s):
         code = pick(s, codes)
@@ -228,13 +268,13 @@
 
             for at, target in enumerate((y3, y1, sibling)):
                 a_copy(tt, half, target, slot + at).start()
-        elif event in ("a0", "b0"):
-            far = int(event == "b0")
+        elif event in ("a3", "b3"):
+            far = int(event == "b3")
             forward(3, far, 0, [sibling], slot)
-            forward(1, far, 0, [y3, sibling], slot + 1)
+            forward(3, far, 1, [y1, sibling], slot + 1)
         elif event in ("a1", "b1"):
             far = int(event == "b1")
-            forward(3, far, 1, [y1, sibling], slot)
+            forward(1, far, 0, [y3, sibling], slot)
             forward(1, far, 1, [sibling], slot + 2)
         else:
             far = int(event == "d")
@@ -408,9 +448,9 @@
             if part == 0:
                 run_first(step)
             elif part == "ev":
-                for event, when in EVENTS:
-
-                    @pl.when(step == when)
+                for event, (when0, when1) in EVENTS:
+
+                    @pl.when(step == (when0 if when0 == when1 else jnp.where(core == 0, when0, when1)))
                     def _():
                         gather(event)
             else:

time: 82.1 us -> 82.2 us (level); the launches traced: 82 us -> 80.7 us
  Pallas kernels: 80.6 us -> 79.3 us
    pallas_call x1, Pallas kernels: 80.6 us -> 79.3 us  [per_device(): pl.pallas_call(kernel, out_shape=pltpu.VMEM((8 * ROWS, WIDTH), F32), in_s...]
where the time goes in v6:
time: 82.2 us; the launch traced here: 80.7 us
  Pallas kernels  79.3 us (96%)
  local copies, waits for them, and re-layouts  1.32 us (2%)
    pallas_call x1, Pallas kernels, per_device(): pl.pallas_call(kernel, out_shape=pltpu.VMEM((8 * ROWS, WIDTH), F32), in_s...  79.3 us

profile of v6, /device:TPU:0, one launch (start us, length us, event | category | flops | bytes accessed | tf_op | source)
XLA Modules:
  0.0 80.7 jit_solution(18062443262063744747)
XLA Ops:
  0.0 79.3 %scaling.1 = f32[512,1024]{1,0:T(8,128)S(1)} custom-call(bf16[1024,4096]{1,0:T(8,128)(2,1)} %act_h.1, bf16[1024,1024]{1,0:T(8,128)(2,1)} %grad_h.1, bf16[4,64,1024]{2,1,0:T(8,128)(2,1)} %ib_h.1, bf16[1,1024,1024]{2,1,0:T(8,128)(2,1)} %ob_h.1), custom_call_target="tpu_custom_call" | custom-call | flops 12000000000 | bytes 16777216 | tf_op jit(solution)/shard_map/scaling/pallas_call | solution.py:484
  79.3 1.3 %copy.6 = f32[512,1024]{1,0:T(8,128)} copy(f32[512,1024]{1,0:T(8,128)S(1)} %scaling.1) | data formatting | bytes 4194304

commit v7 on v6

--- a/solution.py
+++ b/solution.py
@@ -442,6 +442,27 @@
                 encode(reads, xs, s, 2 * UNIT)
                 z_copy(s, part(xs, s, 2 * UNIT, PAIR), part(xr, s, 2 * UNIT, PAIR)).start()
 
+    def gather_left():
+        @pl.loop(0, 28)
+        def _(at):
+            arrived(half_of(t, 0), a_ss.at[at])
+
+        for half in range(2):
+            arrived(ib.at[pl.ds(2 * half, 2)], b_ss.at[half])
+
+    def sums_left(s):
+        tt, own, zfirst = slice_at(s)
+        for mode in range(2):
+            for role in range(2):
+
+                @pl.when((zfirst == mode) & (own == (role == 1)))
+                def _():
+                    count = ((PAIR, UNIT), (UNIT, HALF_UNIT))[mode][role]
+                    for h in range(2):
+                        arrived(part(xs, s, 0, count), x_ss.at[s, h])
+                    if mode or role:
+                        arrived(part(xs, s, 2 * UNIT, PAIR if mode else UNIT), z_ss.at[s])
+
     @pl.loop(0, LAST)
     def _(step):
         for part in SEQUENCE:
@@ -456,26 +477,17 @@
             else:
                 run_later(step, part)
 
-    @pl.loop(0, 28)
-    def _(at):
-        arrived(half_of(t, 0), a_ss.at[at])
-
-    for half in range(2):
-        arrived(ib.at[pl.ds(2 * half, 2)], b_ss.at[half])
-
-    @pl.loop(0, SLICES)
+        @pl.when(step == SLICES)
+        def _():
+            gather_left()
+
+        @pl.when(step >= SLICES)
+        def _():
+            sums_left(step - SLICES)
+
+    @pl.loop(LAST - SLICES, SLICES)
     def _(s):
-        tt, own, zfirst = slice_at(s)
-        for mode in range(2):
-            for role in range(2):
-
-                @pl.when((zfirst == mode) & (own == (role == 1)))
-                def _():
-                    count = ((PAIR, UNIT), (UNIT, HALF_UNIT))[mode][role]
-                    for h in range(2):
-                        arrived(part(xs, s, 0, count), x_ss.at[s, h])
-                    if mode or role:
-                        arrived(part(xs, s, 2 * UNIT, PAIR if mode else UNIT), z_ss.at[s])
+        sums_left(s)
 
 
 def per_device(activations, out_grads, input_basis, output_basis):

time: 82.2 us -> 81.5 us (level)
  no operation moved by 1% of the time
where the time goes in v7:
time: 81.5 us; the launch traced here: 80.2 us
  Pallas kernels  78.8 us (97%)
  local copies, waits for them, and re-layouts  1.32 us (2%)
    pallas_call x1, Pallas kernels, per_device(): pl.pallas_call(kernel, out_shape=pltpu.VMEM((8 * ROWS, WIDTH), F32), in_s...  78.8 us

profile of v7, /device:TPU:0, one launch (start us, length us, event | category | flops | bytes accessed | tf_op | source)
XLA Modules:
  0.0 80.2 jit_solution(3340979074756702089)
XLA Ops:
  0.0 78.8 %scaling.1 = f32[512,1024]{1,0:T(8,128)S(1)} custom-call(bf16[1024,4096]{1,0:T(8,128)(2,1)} %act_h.1, bf16[1024,1024]{1,0:T(8,128)(2,1)} %grad_h.1, bf16[4,64,1024]{2,1,0:T(8,128)(2,1)} %ib_h.1, bf16[1,1024,1024]{2,1,0:T(8,128)(2,1)} %ob_h.1), custom_call_target="tpu_custom_call" | custom-call | flops 12000000000 | bytes 16777216 | tf_op jit(solution)/shard_map/scaling/pallas_call | solution.py:496
  78.8 1.3 %copy.6 = f32[512,1024]{1,0:T(8,128)} copy(f32[512,1024]{1,0:T(8,128)S(1)} %scaling.1) | data formatting | bytes 4194304
